TPU v7x, 128 devices: a whole 4x4x4 slice. The times are simulated.
128 devices in a mesh: box: 16 (over z, x), dir: 8 (over y, core).
Axes of the slice: x: 4, y: 4, z: 4, core: 2. Of those that a mesh axis runs over, the one named last changes fastest.
Arguments:
- currents: bfloat16 [2048, 128, 128], P(('box', 'dir')), may hold values from -6 to 6
- near_blocks: bfloat16 [2048, 8, 128, 256], P(('box', 'dir')), may hold values from -0.375 to 0.375
- near_list: int32 [2048, 8], P(('box', 'dir')), may hold values from 0 to 2047, as said below
- near_count: int32 [2048], P(('box', 'dir')), may hold values from 2 to 8, as said below
- radiation: bfloat16 [1024, 256], replicated, may hold values from -0.375 to 0.375
- child_angle: float32 [2048, 1024], P(('box', 'dir')), may hold values from -3.140625 to 3.140625
- translation: float32 [316, 2, 1024], replicated, may hold values from -0.61237246 to 0.61237246
- inter_src: int32 [128, 6], replicated, may hold values from 0 to 127, as said below
- inter_off: int32 [128, 6], replicated, may hold values from 0 to 315
- inter_count: int32 [128], replicated, may hold values from 2 to 6, as said below
Outputs:
- field: bfloat16 [2048, 128, 128], P(('box', 'dir'))
Inputs may be any that keep to these rules, and one draw needn't show every extreme that they name: `near_list`: entry k of leaf box b names a box at most 8 away from b; entry 0 is b itself and entry 1 lies exactly 8 away. Slots at or beyond near_count[b] of near_list and near_blocks are padding and are not used. `inter_src`: each row names 6 different upper-level boxes, none equal to the row's own. Only the first inter_count[p] slots of row p of inter_src and inter_off are used.
All inputs are finite; a program needn't handle non-finite values.
Results may differ from a plain program's by a relative error of at most 0.006.
Values may be sent and summed in bfloat16 or wider, within the bound.
A program may use at most 128 MiB of HBM per device.

v0:
```python
import jax
import jax.numpy as jnp
from jax import lax
from jax.sharding import PartitionSpec as P

CHILD = 16


def padded(cells, sides, width):
    for axis, dim in sides:
        count = lax.axis_size(axis)
        ends = count - 1
        head = lax.slice_in_dim(cells, 0, width, axis=dim)
        tail = lax.slice_in_dim(cells, cells.shape[dim] - width, cells.shape[dim], axis=dim)
        cells = jnp.concatenate(
            [
                lax.ppermute(tail, axis, [(i, (i + 1) % count) for i in range(ends)]),
                cells,
                lax.ppermute(head, axis, [((i + 1) % count, i) for i in range(ends)]),
            ],
            axis=dim,
        )
    return cells


def turned(values):
    half_width = values.shape[-1] // 2
    return jnp.concatenate([-values[..., half_width:], values[..., :half_width]], axis=-1)


def coefficients(translation, src_rows, off_rows, count_rows, source_width, dir_start, dir_width):
    operators = jnp.take(translation, off_rows, axis=0)
    operators = lax.dynamic_slice_in_dim(operators, dir_start, dir_width, 3)
    slot_ids = jnp.arange(src_rows.shape[1], dtype=jnp.int32)
    live_slot = slot_ids[None, :] < count_rows[:, None]
    source_ids = jnp.arange(source_width, dtype=jnp.int32)
    selector = ((src_rows[:, :, None] == source_ids[None, None, :]) & live_slot[:, :, None]).astype(
        jnp.float32
    )
    return jnp.einsum("tks,tkcq->tscq", selector, operators, precision=lax.Precision.HIGHEST)


def apply_coef(coef, pieces):
    highest = lax.Precision.HIGHEST
    pieces_full = pieces.astype(jnp.float32)
    half_width = pieces.shape[-1] // 2
    real_part = pieces_full[..., :half_width]
    imag_part = pieces_full[..., half_width:]
    real_op = coef[:, :, 0, :]
    imag_op = coef[:, :, 1, :]
    real_out = jnp.einsum("tsq,sqr->tqr", real_op, real_part, precision=highest) - jnp.einsum(
        "tsq,sqr->tqr", imag_op, imag_part, precision=highest
    )
    imag_out = jnp.einsum("tsq,sqr->tqr", real_op, imag_part, precision=highest) + jnp.einsum(
        "tsq,sqr->tqr", imag_op, real_part, precision=highest
    )
    return jnp.concatenate([real_out, imag_out], axis=-1)


def local(
    currents,
    near_blocks,
    near_list,
    near_count,
    radiation,
    child_angle,
    translation,
    inter_src,
    inter_off,
    inter_count,
):
    boxes_dev = currents.shape[0]
    slot_count = near_list.shape[1]
    unknowns = currents.shape[1]
    rhs_width = currents.shape[2] // 2
    directions = radiation.shape[0]
    rim_width = boxes_dev // 2
    dir_count = lax.axis_size("dir")
    dir_rank = lax.axis_index("dir")
    box_rank = lax.axis_index("box")
    first_box = (box_rank * dir_count + dir_rank) * boxes_dev
    parents_dev = boxes_dev // CHILD
    group_size = parents_dev * dir_count
    group_first = box_rank * group_size
    dir_width = directions // dir_count
    dir_start = dir_rank * dir_width
    extended = padded(currents, ((("box", "dir"), 0),), rim_width)
    slot_ids = jnp.arange(slot_count, dtype=jnp.int32)
    live_slot = slot_ids[None, :] < near_count[:, None]
    local_ids = near_list - (first_box - rim_width)
    local_ids = jnp.where(live_slot, local_ids, extended.shape[0])
    neighbours = jnp.take(extended, local_ids, axis=0, mode="fill", fill_value=0)
    split_blocks = near_blocks.reshape(boxes_dev, slot_count, unknowns, 2, unknowns)
    halves = jnp.einsum(
        "bkpcj,bkjr->bcpr", split_blocks, neighbours, preferred_element_type=jnp.float32
    )
    near_part = halves[:, 0] + turned(halves[:, 1])
    cos_all = jnp.cos(child_angle)[:, :, None]
    sin_all = jnp.sin(child_angle)[:, :, None]
    split_radiation = radiation.reshape(directions, 2, unknowns)
    leaf_halves = jnp.einsum(
        "qcj,bjr->bcqr", split_radiation, currents, preferred_element_type=jnp.float32
    )
    leaf_terms = leaf_halves[:, 0] + turned(leaf_halves[:, 1])
    rotated = cos_all * leaf_terms + sin_all * turned(leaf_terms)
    local_pattern = jnp.sum(
        rotated.reshape(parents_dev, CHILD, directions, 2 * rhs_width), axis=1
    ).astype(jnp.bfloat16)
    group_slice = lax.all_to_all(local_pattern, "dir", split_axis=1, concat_axis=0, tiled=True)
    src_rows = lax.dynamic_slice_in_dim(inter_src, group_first, group_size, 0)
    off_rows = lax.dynamic_slice_in_dim(inter_off, group_first, group_size, 0)
    count_rows = lax.dynamic_slice_in_dim(inter_count, group_first, group_size, 0)
    pieces = lax.all_gather(group_slice, "box", axis=0, tiled=True)
    coef = coefficients(
        translation, src_rows, off_rows, count_rows, pieces.shape[0], dir_start, dir_width
    )
    incoming_slice = apply_coef(coef, pieces).astype(jnp.bfloat16)
    incoming = lax.all_to_all(incoming_slice, "dir", split_axis=0, concat_axis=1, tiled=True)
    incoming_full = jnp.repeat(incoming, CHILD, axis=0).astype(jnp.float32)
    shifted = (cos_all * incoming_full - sin_all * turned(incoming_full)).astype(jnp.bfloat16)
    mixed_terms = jnp.einsum("qj,bqr->bjr", radiation, shifted, preferred_element_type=jnp.float32)
    far_real = mixed_terms[:, :unknowns, :rhs_width] + mixed_terms[:, unknowns:, rhs_width:]
    far_imag = mixed_terms[:, :unknowns, rhs_width:] - mixed_terms[:, unknowns:, :rhs_width]
    far_part = jnp.concatenate([far_real, far_imag], axis=-1)
    return (near_part + far_part).astype(jnp.bfloat16)


def solution(mesh):
    return jax.shard_map(
        local,
        mesh=mesh,
        in_specs=(
            P(("box", "dir"), None, None),
            P(("box", "dir"), None, None, None),
            P(("box", "dir"), None),
            P(("box", "dir")),
            P(),
            P(("box", "dir"), None),
            P(),
            P(),
            P(),
            P(),
        ),
        out_specs=P(("box", "dir"), None, None),
        check_vma=False,
    )
```

profile of v0, /device:TPU:1, one launch (start us, length us, event | category | flops | bytes accessed | tf_op | source)
XLA Modules:
  0.0 186.5 jit_solution(17364101178362907800)
XLA Ops:
  6.5 3.7 %convolution_bitcast_fusion = f32[16,2,1024,128]{2,3,1,0:T(8,128)S(1)} fusion(bf16[16,128,128]{2,1,0:T(8,128)(2,1)} %param.10, bf16[1024,256]{1,0:T(8,128)(2,1)} %param.14), kind=kOutput, calls=%fused_computation.2 | convolution fusion | flops 1073741824 | bytes 17825792 | tf_op jit(solution)/shard_map/qcj,bjr->bcqr/dot_general | solution.py:101
  10.3 5.7 %copy-done.2 = f32[16,2,1024,128]{2,3,1,0:T(8,128)} copy-done((f32[16,2,1024,128]{2,3,1,0:T(8,128)}, f32[16,2,1024,128]{2,3,1,0:T(8,128)S(1)}, u32[]{:S(2)}) %copy-start.2) | copy-done | bytes 16777240
  16.0 4.1 %slice_bitcast_fusion = f32[16,1024,128]{1,2,0:T(8,128)} fusion(f32[16,2,1024,128]{2,3,1,0:T(8,128)S(1)} %convolution_bitcast_fusion), kind=kLoop, calls=%fused_computation.6 | loop fusion | bytes 16777216 | tf_op jit(solution)/shard_map/squeeze | solution.py:104
  20.1 10.6 %slice_negate_fusion.1 = (f32[16,1024,64]{1,2,0:T(8,128)}, f32[1,16,1024,64]{2,3,1,0:T(8,128)}, f32[1,16,1024,64]{2,3,1,0:T(8,128)}, f32[16,1024,64]{1,2,0:T(8,128)}) fusion(f32[16,1024,128]{1,2,0:T(8,128)} %slice_bitcast_fusion), kind=kLoop, calls=%fused_computation.19 | loop fusion | flops 1048576 | bytes 25165824 | tf_op jit(solution)/shard_map/neg | solution.py:28
  30.7 6.8 %maximum_add_fusion.1 = f32[16,1024,128]{1,2,0:T(8,128)S(1)} fusion(f32[16,1024,64]{1,2,0:T(8,128)} %get-tuple-element.14, f32[16,1024,64]{1,2,0:T(8,128)} %get-tuple-element.11, f32[16,2,1024,128]{2,3,1,0:T(8,128)} %copy-done.2), kind=kLoop, calls=%fused_computation.11 | loop fusion | flops 4194304 | bytes 25165824 | tf_op jit(solution)/shard_map/add | solution.py:104
  37.6 5.1 %fusion.8 = (f32[1,16,1024,64]{2,3,1,0:T(8,128)}, f32[1,16,1024,64]{2,3,1,0:T(8,128)}) fusion(f32[16,1024,128]{1,2,0:T(8,128)S(1)} %maximum_add_fusion.1), kind=kLoop, calls=%fused_computation.18 | loop fusion | flops 1048576 | bytes 16777216 | tf_op jit(solution)/shard_map/concatenate | solution.py:28
  42.7 0.2 fusion.47
  42.9 1.0 copy-done.5
  43.9 7.7 %fusion.5 = bf16[1024,128]{0,1:T(8,128)(2,1)S(1)} fusion(f32[1,16,1024,64]{2,3,1,0:T(8,128)S(1)} %copy-done.5, f32[1,16,1024,64]{2,3,1,0:T(8,128)S(1)} %copy-done.4, f32[1,16,1024,64]{2,3,1,0:T(8,128)} %get-tuple-element.10, f32[1,16,1024,64]{2,3,1,0:T(8,128)} %get-tuple-element.9, f32[16,2,1024,128]{2,3,1,0:T(8,128)} %copy-done.2, ...), kind=kLoop, calls=%fused_computation.10 | loop fusion | flops 14548992 | bytes 25559040 | tf_op jit(solution)/shard_map/reduce_sum | solution.py:106
  51.7 1.1 copy.81
  52.8 0.5 broadcast.52
  53.3 3.1 %reduce.1 = bf16[1024,128]{1,0:T(8,128)(2,1)S(1)} reduce(bf16[1024,1,128]{2,1,0:T(2,128)(2,1)} %bitcast.108, bf16[]{:T(256)} %broadcast.52), dimensions={1}, to_apply=%bitcast.88.reduce_sub_computation | reduce | bytes 524290
  56.4 0.8 reshape.176
  57.1 12.5 %all_to_all.21 = bf16[8,2,8192]{2,1,0:T(2,128)(2,1)S(1)} all-to-all(bf16[8,2,8192]{2,1,0:T(2,128)(2,1)} %reshape.176), channel_id=1, replica_groups=mesh['box'=16,'dir'=8] {'dir'}, dimensions={0} | all-to-all | bytes 524288 | tf_op jit(solution)/shard_map/all_to_all | solution.py:109
  69.6 1.0 reshape.177
  70.6 1.8 copy.103
  72.4 0.0 all-gather.2.cloned.1.call-update
  72.4 0.9 fusion.46
  73.3 3.1 %collective-permute-start = (bf16[8,128,128]{2,1,0:T(8,128)(2,1)}, bf16[8,128,128]{2,1,0:T(8,128)(2,1)}, u32[]{:S(2)}, u32[]{:S(2)}) collective-permute-start(bf16[8,128,128]{2,1,0:T(8,128)(2,1)} %get-tuple-element.23), channel_id=1, source_target_pairs={{0,1},{1,2},{2,3},{3,4},{4,5},{5,6},{6,7},{7,8},{8,9},{9,10},{10,1... | collective-permute-start | bytes 786440 | tf_op jit(solution)/shard_map/ppermute | solution.py:17
  76.4 2.1 %collective-permute-start.1 = (bf16[8,128,128]{2,1,0:T(8,128)(2,1)}, bf16[8,128,128]{2,1,0:T(8,128)(2,1)}, u32[]{:S(2)}, u32[]{:S(2)}) collective-permute-start(bf16[8,128,128]{2,1,0:T(8,128)(2,1)} %get-tuple-element.24), channel_id=1, source_target_pairs={{1,0},{2,1},{3,2},{4,3},{5,4},{6,5},{7,6},{8,7},{9,8},{10,9},{11,1... | collective-permute-start | bytes 786440 | tf_op jit(solution)/shard_map/ppermute | solution.py:19
  78.5 0.1 compare_and_fusion
  78.6 0.1 copy.85
  78.7 0.1 reshape.156
  78.8 0.1 copy.84
  78.9 0.1 constant_dynamic-slice_fusion.1
  78.9 0.1 copy.83
  79.0 0.1 dynamic_slice.13
  79.1 1.0 gather_fusion.1
  80.1 0.1 iota_compare_fusion.1
  80.2 0.8 fusion.33
  81.0 0.1 slice_bitcast_fusion.4
  81.1 1.0 copy.87
  82.1 1.0 copy.89
  83.1 0.1 copy.74
  83.2 0.1 reshape.148
  83.3 0.1 copy.73
  83.4 1.0 collective-permute-done.1
  84.4 1.2 pad_maximum_fusion
  85.6 3.1 %gather_fusion = bf16[128,128,128]{2,1,0:T(8,128)(2,1)} fusion(bf16[32,128,128]{2,1,0:T(8,128)(2,1)S(1)} %pad_maximum_fusion, s32[1024]{0:T(1024)S(1)} %pad_clamp_fusion.1), kind=kCustom, calls=%fused_computation | custom fusion | bytes 8389120 | tf_op jit(solution)/shard_map/jit(_take)/gather | solution.py:92
  88.6 6.5 %copy.75 = bf16[16,8,128,128]{2,3,1,0:T(8,128)(2,1)} copy(bf16[16,8,128,128]{3,2,1,0:T(8,128)(2,1)} %bitcast.105) | data formatting | bytes 8388608 | tf_op jit(solution)/shard_map/jit(_take)/gather | solution.py:92
  95.1 8.8 %fusion.15 = f32[16,2,128,128]{2,3,1,0:T(8,128)} fusion(bf16[16,8,128,128]{2,3,1,0:T(8,128)(2,1)} %copy.75, pred[16,8]{1,0:T(8,128)(4,1)S(1)} %copy.73, bf16[16,8,128,256]{3,2,1,0:T(8,128)(2,1)} %param.11), kind=kOutput, calls=%fused_computation.25 | convolution fusion | flops 1075838976 | bytes 14680192 | tf_op jit(solution)/shard_map/bkpcj,bkjr->bcpr/dot_general | solution.py:94
  103.9 22.3 %all-gather.2.cloned.1.call-done = bf16[128,128,128]{2,1,0:T(8,128)(2,1)} async-done(((bf16[8,128,128]{2,1,0:T(8,128)(2,1)}), bf16[128,128,128]{2,1,0:T(8,128)(2,1)}) %all-gather.2.cloned.1.call-update) | async-done | bytes 4194320 | tf_op jit(solution)/shard_map/all_gather | solution.py:113
  126.2 7.5 %fusion.45 = (bf16[128,128,64]{2,1,0:T(8,128)(2,1)}, bf16[128,128,64]{2,1,0:T(8,128)(2,1)}) fusion(bf16[128,128,128]{2,1,0:T(8,128)(2,1)} %all-gather.2.cloned.1.call-done), kind=kLoop, calls=%fused_computation.76 | loop fusion | bytes 8388608 | tf_op jit(solution)/shard_map/slice | solution.py:47
  133.8 5.6 %copy.106 = bf16[128,128,64]{0,2,1:T(8,128)(2,1)S(1)} copy(bf16[128,128,64]{2,1,0:T(8,128)(2,1)} %get-tuple-element.15) | data formatting | bytes 4194304
  139.4 6.6 %copy.107 = bf16[128,128,64]{0,2,1:T(8,128)(2,1)} copy(bf16[128,128,64]{2,1,0:T(8,128)(2,1)} %get-tuple-element.16) | data formatting | bytes 4194304
  146.0 3.3 %fusion.48 = f32[128,64,8]{1,2,0:T(8,128)S(1)} fusion(bf16[128,128,64]{0,2,1:T(8,128)(2,1)S(1)} %copy.106, f32[8,128,128]{1,0,2:T(8,128)S(1)} %copy-done.8), kind=kOutput, calls=%fused_computation.79 | convolution fusion | flops 100663296 | bytes 2883584 | tf_op jit(solution)/shard_map/tsq,sqr->tqr/dot_general | solution.py:51
  149.4 4.9 %fusion.49 = f32[128,64,8]{1,2,0:T(8,128)S(1)} fusion(bf16[128,128,64]{0,2,1:T(8,128)(2,1)} %copy.107, f32[8,128,128]{1,0,2:T(8,128)S(1)} %copy-done.8), kind=kOutput, calls=%fused_computation.80 | convolution fusion | flops 100663296 | bytes 2883584 | tf_op jit(solution)/shard_map/tsq,sqr->tqr/dot_general | solution.py:54
  154.3 3.4 %fusion.26 = bf16[8,128,64]{2,0,1:T(8,128)(2,1)S(1)} fusion(f32[128,64,8]{1,2,0:T(8,128)S(1)} %fusion.48, bf16[128,128,64]{0,2,1:T(8,128)(2,1)S(1)} %copy-done.3, f32[8,128,128]{1,0,2:T(8,128)S(1)} %copy-done.7), kind=kOutput, calls=%fused_computation.32 | convolution fusion | flops 100794368 | bytes 3014656 | tf_op jit(solution)/shard_map/tsq,sqr->tqr/dot_general | solution.py:51
  157.7 3.4 %fusion.25 = bf16[8,128,64]{2,0,1:T(8,128)(2,1)S(1)} fusion(f32[128,64,8]{1,2,0:T(8,128)S(1)} %fusion.49, bf16[128,128,64]{0,2,1:T(8,128)(2,1)S(1)} %copy.106, f32[8,128,128]{1,0,2:T(8,128)S(1)} %copy-done.7), kind=kOutput, calls=%fused_computation.31 | convolution fusion | flops 100794368 | bytes 3014656 | tf_op jit(solution)/shard_map/tsq,sqr->tqr/dot_general | solution.py:54
  161.0 0.2 pad_maximum_fusion.1
  161.2 0.7 copy.92
  162.0 5.0 %all-to-all-start.1 = ((bf16[8,128,128]{2,1,0:T(8,128)(2,1)}), bf16[8,128,128]{2,1,0:T(8,128)(2,1)S(1)}, u32[]{:S(2)}, u32[]{:S(2)}) async-start(bf16[8,128,128]{2,1,0:T(8,128)(2,1)} %copy.92), calls=%async_computation.1 | async-start | bytes 524288 | tf_op jit(solution)/shard_map/all_to_all | solution.py:118
  166.9 2.3 %slice_bitcast_fusion.2 = f32[16,128,128]{1,2,0:T(8,128)} fusion(f32[16,2,128,128]{2,3,1,0:T(8,128)} %fusion.15), kind=kLoop, calls=%fused_computation.33 | loop fusion | bytes 2097152 | tf_op jit(solution)/shard_map/squeeze | solution.py:97
  169.2 4.2 %all-to-all-done.1 = bf16[8,128,128]{2,1,0:T(8,128)(2,1)S(1)} async-done(((bf16[8,128,128]{2,1,0:T(8,128)(2,1)}), bf16[8,128,128]{2,1,0:T(8,128)(2,1)S(1)}, u32[]{:S(2)}, u32[]{:S(2)}) %all-to-all-start.1) | async-done | bytes 262176 | tf_op jit(solution)/shard_map/all_to_all | solution.py:118
  173.4 0.1 bitcast_convert_fusion
  173.5 0.2 copy.93
  173.7 0.2 copy.95
  173.9 0.5 reshape.143
  174.4 0.5 reshape.144
  175.0 1.8 fusion.20
  176.8 0.3 slice_add_fusion
  177.1 1.3 copy-done.10
  178.4 0.2 fusion.29
  178.6 1.0 copy.96
  (48 shorter events, 0.2 us)
Async XLA Ops:
  6.5 72.6 %copy-start = (f32[316,2,1024]{2,1,0:T(2,128)S(1)}, f32[316,2,1024]{2,1,0:T(2,128)}, u32[]{:S(2)}) copy-start(f32[316,2,1024]{2,1,0:T(2,128)} %param.16) | copy-start | bytes 7766020
  6.5 119.7 %all-gather.2.cloned.1.call-start = ((), (), s32[]{:S(2)}) async-start(), calls=%async_computation.2 | async-start | bytes 4456448 | tf_op jit(solution)/shard_map/all_gather | solution.py:113
  10.3 5.7 %copy-start.2 = (f32[16,2,1024,128]{2,3,1,0:T(8,128)}, f32[16,2,1024,128]{2,3,1,0:T(8,128)S(1)}, u32[]{:S(2)}) copy-start(f32[16,2,1024,128]{2,3,1,0:T(8,128)S(1)} %convolution_bitcast_fusion) | copy-start | bytes 50331652
  37.5 5.1 %copy-start.16 = (f32[16,1024]{1,0:T(8,128)S(1)}, f32[16,1024]{1,0:T(8,128)}, u32[]{:S(2)}) copy-start(f32[16,1024]{1,0:T(8,128)} %param.15) | copy-start | bytes 196612
  37.5 5.4 %copy-start.4 = (f32[1,16,1024,64]{2,3,1,0:T(8,128)S(1)}, f32[1,16,1024,64]{2,3,1,0:T(8,128)}, u32[]{:S(2)}) copy-start(f32[1,16,1024,64]{2,3,1,0:T(8,128)} %get-tuple-element.12) | copy-start | bytes 12582916
  37.5 6.4 %copy-start.5 = (f32[1,16,1024,64]{2,3,1,0:T(8,128)S(1)}, f32[1,16,1024,64]{2,3,1,0:T(8,128)}, u32[]{:S(2)}) copy-start(f32[1,16,1024,64]{2,3,1,0:T(8,128)} %get-tuple-element.13) | copy-start | bytes 12582916
  42.9 8.8 %copy-start.12 = (f32[16,1024]{1,0:T(8,128)}, f32[16,1024]{1,0:T(8,128)S(1)}, u32[]{:S(2)}) copy-start(f32[16,1024]{1,0:T(8,128)S(1)} %get-tuple-element.25) | copy-start | bytes 196612
  42.9 8.8 %copy-start.14 = (f32[16,1024]{1,0:T(8,128)}, f32[16,1024]{1,0:T(8,128)S(1)}, u32[]{:S(2)}) copy-start(f32[16,1024]{1,0:T(8,128)S(1)} %get-tuple-element.26) | copy-start | bytes 196612
  51.7 20.7 %copy-start.6 = (bf16[16,128,128]{2,1,0:T(8,128)(2,1)S(1)}, bf16[16,128,128]{2,1,0:T(8,128)(2,1)}, u32[]{:S(2)}) copy-start(bf16[16,128,128]{2,1,0:T(8,128)(2,1)} %param.10) | copy-start | bytes 1572868
  51.7 26.8 %copy-start.17 = (s32[128,6]{0,1:T(8,128)S(1)}, s32[128,6]{0,1:T(8,128)}, u32[]{:S(2)}) copy-start(s32[128,6]{0,1:T(8,128)} %param.18) | copy-start | bytes 9220
  51.7 27.2 %copy-start.18 = (s32[128,6]{0,1:T(8,128)S(1)}, s32[128,6]{0,1:T(8,128)}, u32[]{:S(2)}) copy-start(s32[128,6]{0,1:T(8,128)} %param.17) | copy-start | bytes 9220
  51.7 27.3 %copy-start.21 = (s32[128]{0:T(128)S(1)}, s32[128]{0:T(128)}, u32[]{:S(2)}) copy-start(s32[128]{0:T(128)} %param.19) | copy-start | bytes 1540
  70.6 12.5 %copy-start.19 = (s32[16,8]{0,1:T(8,128)S(1)}, s32[16,8]{0,1:T(8,128)}, u32[]{:S(2)}) copy-start(s32[16,8]{0,1:T(8,128)} %param.12) | copy-start | bytes 1540
  70.6 12.5 %copy-start.20 = (s32[16]{0:T(128)S(1)}, s32[16]{0:T(128)}, u32[]{:S(2)}) copy-start(s32[16]{0:T(128)} %param.13) | copy-start | bytes 196
  73.3 10.1 %collective-permute-start = (bf16[8,128,128]{2,1,0:T(8,128)(2,1)}, bf16[8,128,128]{2,1,0:T(8,128)(2,1)}, u32[]{:S(2)}, u32[]{:S(2)}) collective-permute-start(bf16[8,128,128]{2,1,0:T(8,128)(2,1)} %get-tuple-element.23), channel_id=1, source_target_pairs={{0,1},{1,2},{2,3},{3,4},{4,5},{5,6},{6,7},{7,8},{8,9},{9,10},{10,1... | collective-permute-start | bytes 786440 | tf_op jit(solution)/shard_map/ppermute | solution.py:17
  76.4 8.0 %collective-permute-start.1 = (bf16[8,128,128]{2,1,0:T(8,128)(2,1)}, bf16[8,128,128]{2,1,0:T(8,128)(2,1)}, u32[]{:S(2)}, u32[]{:S(2)}) collective-permute-start(bf16[8,128,128]{2,1,0:T(8,128)(2,1)} %get-tuple-element.24), channel_id=1, source_target_pairs={{1,0},{2,1},{3,2},{4,3},{5,4},{6,5},{7,6},{8,7},{9,8},{10,9},{11,1... | collective-permute-start | bytes 786440 | tf_op jit(solution)/shard_map/ppermute | solution.py:19
  139.4 6.6 %copy-start.8 = (f32[8,128,128]{1,0,2:T(8,128)S(1)}, f32[8,128,128]{1,0,2:T(8,128)}, u32[]{:S(2)}) copy-start(f32[8,128,128]{1,0,2:T(8,128)} %copy.87) | copy-start | bytes 1572868
  146.0 8.3 %copy-start.3 = (bf16[128,128,64]{0,2,1:T(8,128)(2,1)S(1)}, bf16[128,128,64]{0,2,1:T(8,128)(2,1)}, u32[]{:S(2)}) copy-start(bf16[128,128,64]{0,2,1:T(8,128)(2,1)} %copy.107) | copy-start | bytes 6291460
  146.0 8.3 %copy-start.7 = (f32[8,128,128]{1,0,2:T(8,128)S(1)}, f32[8,128,128]{1,0,2:T(8,128)}, u32[]{:S(2)}) copy-start(f32[8,128,128]{1,0,2:T(8,128)} %copy.89) | copy-start | bytes 1572868
  162.0 11.5 %all-to-all-start.1 = ((bf16[8,128,128]{2,1,0:T(8,128)(2,1)}), bf16[8,128,128]{2,1,0:T(8,128)(2,1)S(1)}, u32[]{:S(2)}, u32[]{:S(2)}) async-start(bf16[8,128,128]{2,1,0:T(8,128)(2,1)} %copy.92), calls=%async_computation.1 | async-start | bytes 524288 | tf_op jit(solution)/shard_map/all_to_all | solution.py:118
  173.9 1.1 copy-start.11
  173.9 1.1 copy-start.13
  173.9 1.1 copy-start.15
  175.0 1.8 copy-start.9
  175.0 4.6 %copy-start.1 = (f32[316,2,1024]{2,1,0:T(2,128)S(1)}, f32[316,2,1024]{2,1,0:T(2,128)}, u32[]{:S(2)}) copy-start(f32[316,2,1024]{2,1,0:T(2,128)} %param.16) | copy-start | bytes 7766020
  176.8 1.6 copy-start.10
Sparse Core Ops, SparseCore 0:
  72.5 53.6 all-gather.1
where the time goes:
time: 187 us; the launch traced here: 186 us
  local copies, waits for them, and re-layouts  57.1 us (31%)
  other arithmetic  35.3 us (19%)
  matrix products  30.1 us (16%)
  waiting for transfers between devices  27.6 us (15%)
  between operations  13.8 us (7%)
  blocking collectives  12.5 us (7%)
  starting transfers between devices  10.2 us (5%)
    unnamed x50, local copies, waits for them, and re-layouts  24.4 us
    all_gather x1, waiting for transfers between devices, local(): pieces = lax.all_gather(group_slice, 'box', axis=0, tiled=True)  22.3 us
    all_to_all x1, blocking collectives, local(): lax.all_to_all(local_pattern, 'dir', split_axis=1, concat_axis=0, tiled=T...  12.5 us
    neg x2, other arithmetic, turned(): -values[..., half_width:]  10.6 us
    gather x2, local copies, waits for them, and re-layouts, local(): jnp.take(extended, local_ids, axis=0, mode='fill', fill_value=0)  9.57 us
    dot_general x1, matrix products, local(): jnp.einsum('bkpcj,bkjr->bcpr', split_blocks, neighbours, preferred_elemen...  8.8 us
    reduce_sum x1, other arithmetic, local(): jnp.sum(rotated.reshape(parents_dev, CHILD, directions, 2 * rhs_width), a...  7.71 us
    slice x1, local copies, waits for them, and re-layouts, apply_coef(): real_part = pieces_full[..., :half_width]  7.51 us
  transfers between devices with their start and end apart: 4, of which 3 were waited for; matrix products, arithmetic and copies ran while one was open for 15% of the time, Pallas kernels for 0%

commit v1 on v0

v1 whole, which is shorter than its diff:
```python
import functools

import jax
import jax.numpy as jnp
from jax import lax
from jax.experimental import pallas as pl
from jax.experimental.pallas import tpu as pltpu
from jax.sharding import PartitionSpec as P

MESH = pl.DeviceIdType.MESH
F32 = jnp.float32
BF16 = jnp.bfloat16
NT = (((1,), (1,)), ((), ()))


def sincos(angle):
    h = angle * 0.5
    z = h * h
    s = -1.0 / 1307674368000.0
    for inv in (6227020800.0, -39916800.0, 362880.0, -5040.0, 120.0, -6.0, 1.0):
        s = s * z + 1.0 / inv
    s = s * h
    c = 1.0 / 20922789888000.0
    for inv in (-87178291200.0, 479001600.0, -3628800.0, 40320.0, -720.0, 24.0, -2.0, 1.0):
        c = c * z + 1.0 / inv
    return 2.0 * s * c, 1.0 - 2.0 * s * s


def iota2(rows, columns):
    return (
        lax.broadcasted_iota(jnp.int32, (rows, columns), 0),
        lax.broadcasted_iota(jnp.int32, (rows, columns), 1),
    )


def kernel(
    nbox,
    ndir,
    ids,
    src,
    off,
    x_hbm,
    z_hbm,
    a_hbm,
    ang_hbm,
    tr_hbm,
    out_ref,
    xext,
    zbuf,
    a_ref,
    ang,
    trans,
    cosb,
    sinb,
    lhs,
    send1,
    recv1,
    recv2,
    send3,
    recv3,
    recv4,
    near,
    inc,
    shf,
    load_sem,
    own_sem,
    s1,
    r1,
    s2,
    r2,
    s3,
    r3,
    s4,
    r4,
    sh,
    rh,
):
    box = lax.axis_index("box")
    me = lax.axis_index("dir")
    chips = ndir // 2
    my_y = me // 2
    boxes = x_hbm.shape[0]
    half = boxes // 2

    rank = box * ndir + me
    total = nbox * ndir
    right = lax.rem(rank + 1, total)
    left = lax.rem(rank + total - 1, total)
    right_id = (right // ndir, lax.rem(right, ndir))
    left_id = (left // ndir, lax.rem(left, ndir))

    barrier = pltpu.get_barrier_semaphore()
    for s in range(1, ndir):
        pl.semaphore_signal(
            barrier, inc=1, device_id=(box, lax.rem(me + s, ndir)), device_id_type=MESH
        )
    for s in range(1, nbox):
        pl.semaphore_signal(
            barrier, inc=1, device_id=(lax.rem(box + s, nbox), me), device_id_type=MESH
        )
    for there in (left_id, right_id):
        pl.semaphore_signal(barrier, inc=1, device_id=there, device_id_type=MESH)

    load_x = pltpu.make_async_copy(x_hbm, xext.at[pl.ds(half, boxes)], load_sem.at[0])
    load_a = pltpu.make_async_copy(a_hbm, a_ref, load_sem.at[1])
    load_g = pltpu.make_async_copy(ang_hbm, ang, load_sem.at[2])
    load_t = pltpu.make_async_copy(
        tr_hbm.at[:, :, pl.ds(pl.multiple_of(me * 128, 128), 128)],
        trans.at[pl.ds(0, tr_hbm.shape[0])],
        load_sem.at[3],
    )
    load_z = pltpu.make_async_copy(z_hbm, zbuf, load_sem.at[4])
    load_x.start()
    load_g.start()
    load_a.start()
    load_t.start()
    load_z.start()

    xext[2 * boxes] = jnp.zeros((128, 128), BF16)
    trans[pl.ds(tr_hbm.shape[0], 4)] = jnp.zeros((4, 2, 128), F32)

    row, col = iota2(128, 128)
    within = lax.rem(row, 8)
    natural = 4 * lax.div(row, 8) + lax.rem(within, 4) + 64 * lax.div(within, 4)
    perm = jnp.where(col == natural, 1.0, 0.0).astype(BF16)
    within_t = lax.rem(col, 8)
    natural_t = 4 * lax.div(col, 8) + lax.rem(within_t, 4) + 64 * lax.div(within_t, 4)
    perm_t = jnp.where(row == natural_t, 1.0, 0.0).astype(BF16)
    row2, col2 = iota2(256, 128)
    spread = jnp.where(row2 == col2, 1.0, 0.0)
    spread = jnp.where((row2 >= 128) & (row2 < 192) & (col2 == row2 - 64), -1.0, spread)
    spread = jnp.where((row2 >= 192) & (col2 == row2 - 192), 1.0, spread).astype(BF16)

    load_g.wait()
    for y in range(chips):
        sn, cs = sincos(ang[:, y * 256 : (y + 1) * 256])
        sinb[y] = sn
        cosb[y] = cs

    load_x.wait()
    for i in range(boxes // 4):
        four = xext[half + 4 * i : half + 4 * i + 4].reshape(512, 128)
        turned = lax.dot_general(spread, four, NT, preferred_element_type=F32).astype(BF16)
        for j in range(4):
            rows = slice((4 * i + j) * 128, (4 * i + j + 1) * 128)
            lhs[rows, 0:128] = turned[0:128, j * 128 : (j + 1) * 128]
            lhs[rows, 128:256] = turned[128:256, j * 128 : (j + 1) * 128]

    load_a.wait()
    pl.semaphore_wait(barrier, ndir + nbox)

    def copy1(j):
        return pltpu.make_async_remote_copy(
            src_ref=send1.at[j],
            dst_ref=recv1.at[me],
            send_sem=s1.at[j],
            recv_sem=r1.at[me],
            device_id=(box, j),
            device_id_type=MESH,
        )

    def wait1(j):
        return pltpu.make_async_remote_copy(
            src_ref=send1.at[j],
            dst_ref=recv1.at[j],
            send_sem=s1.at[j],
            recv_sem=r1.at[j],
            device_id=(box, j),
            device_id_type=MESH,
        )

    own1 = pltpu.make_async_copy(send1.at[me], recv1.at[me], own_sem.at[0])

    def pattern_step(s, carry):
        y = lax.rem(my_y + 1 + s, chips)
        block = a_ref[pl.ds(pl.multiple_of(y * 256, 256), 256), :]
        re = jnp.zeros((64, 256), F32)
        im = jnp.zeros((64, 256), F32)
        for i in range(boxes // 4):
            terms = lax.dot_general(
                lhs[512 * i : 512 * (i + 1), :], block, NT, preferred_element_type=F32
            )
            for j in range(4):
                b = 4 * i + j
                c = cosb[y, b : b + 1, :]
                d = sinb[y, b : b + 1, :]
                tre = terms[j * 128 : j * 128 + 64]
                tim = terms[j * 128 + 64 : (j + 1) * 128]
                re = re + (c * tre - d * tim)
                im = im + (d * tre + c * tim)
        pat = jnp.concatenate([re, im], axis=0).astype(BF16)
        pat = jnp.dot(perm, pat, preferred_element_type=F32)
        for h in range(2):
            j = 2 * y + h
            send1[j] = pat[:, h * 128 : (h + 1) * 128].reshape(nbox, 8, 128).astype(BF16)

            @pl.when(j != me)
            def _():
                copy1(j).start()

            @pl.when(j == me)
            def _():
                own1.start()

        return carry

    lax.fori_loop(0, chips, pattern_step, 0)

    to_right = pltpu.make_async_remote_copy(
        src_ref=xext.at[pl.ds(boxes, half)],
        dst_ref=xext.at[pl.ds(0, half)],
        send_sem=sh.at[0],
        recv_sem=rh.at[0],
        device_id=right_id,
        device_id_type=MESH,
    )
    to_left = pltpu.make_async_remote_copy(
        src_ref=xext.at[pl.ds(half, half)],
        dst_ref=xext.at[pl.ds(half + boxes, half)],
        send_sem=sh.at[1],
        recv_sem=rh.at[1],
        device_id=left_id,
        device_id_type=MESH,
    )

    own1.wait()
    for s in range(1, ndir):
        wait1(lax.rem(me + s, ndir)).wait_recv()

    def copy2(g, slot):
        return pltpu.make_async_remote_copy(
            src_ref=recv1.at[:, g],
            dst_ref=recv2.at[pl.ds(slot * 8, 8)],
            send_sem=s2.at[g],
            recv_sem=r2.at[slot],
            device_id=(g, me),
            device_id_type=MESH,
        )

    own2 = pltpu.make_async_copy(recv1.at[:, box], recv2.at[pl.ds(box * 8, 8)], own_sem.at[1])
    for s in range(1, nbox):
        copy2(lax.rem(box + s, nbox), box).start()
    own2.start()
    to_right.start()
    to_left.start()

    load_t.wait()
    own2.wait()
    for s in range(1, nbox):
        g = lax.rem(box + s, nbox)
        copy2(g, g).wait_recv()

    def copy3(g, slot):
        return pltpu.make_async_remote_copy(
            src_ref=send3.at[pl.ds(g * 8, 8)],
            dst_ref=recv3.at[slot],
            send_sem=s3.at[g],
            recv_sem=r3.at[slot],
            device_id=(g, me),
            device_id_type=MESH,
        )

    own3 = pltpu.make_async_copy(send3.at[pl.ds(box * 8, 8)], recv3.at[box], own_sem.at[2])
    sign = jnp.where(lax.broadcasted_iota(jnp.int32, (8, 128), 0) < 4, -1.0, 1.0)
    slots = src.shape[0] // (nbox * ndir)

    def translate_step(s, carry):
        g = lax.rem(box + 1 + s, nbox)
        for i in range(ndir):
            t = g * ndir + i
            straight = jnp.zeros((8, 128), F32)
            crossed = jnp.zeros((8, 128), F32)
            for k in range(slots):
                v = recv2[src[t * slots + k]].astype(F32)
                tau = trans[off[t * slots + k]]
                straight = straight + tau[0:1] * v
                crossed = crossed + tau[1:2] * v
            total_in = straight + sign * pltpu.roll(crossed, 4, 0)
            send3[t] = total_in.astype(BF16)

        @pl.when(g != box)
        def _():
            copy3(g, box).start()

        @pl.when(g == box)
        def _():
            own3.start()

        return carry

    lax.fori_loop(0, nbox, translate_step, 0)

    load_z.wait()
    to_right.wait_recv()
    to_left.wait_recv()

    def near_step(b, carry):
        gathered = jnp.concatenate([xext[ids[b * 8 + k]] for k in range(8)], axis=0)
        zr = jnp.concatenate([zbuf[b, k, :, 0:128] for k in range(8)], axis=1)
        zi = jnp.concatenate([zbuf[b, k, :, 128:256] for k in range(8)], axis=1)
        both = jnp.dot(
            jnp.concatenate([zr, zi], axis=0), gathered, preferred_element_type=F32
        )
        cross = pltpu.roll(both[128:256], 64, 1)
        lane = lax.broadcasted_iota(jnp.int32, (128, 128), 1)
        near[b] = both[0:128] + jnp.where(lane < 64, -cross, cross)
        return carry

    lax.fori_loop(0, boxes, near_step, 0)

    own3.wait()
    for s in range(1, nbox):
        g = lax.rem(box + s, nbox)
        copy3(g, g).wait_recv()

    def copy4(j, slot):
        return pltpu.make_async_remote_copy(
            src_ref=recv3.at[:, j],
            dst_ref=recv4.at[slot],
            send_sem=s4.at[j],
            recv_sem=r4.at[slot],
            device_id=(box, j),
            device_id_type=MESH,
        )

    own4 = pltpu.make_async_copy(recv3.at[:, me], recv4.at[me], own_sem.at[3])
    for s in range(1, ndir):
        copy4(lax.rem(me + s, ndir), me).start()
    own4.start()
    own4.wait()
    for s in range(1, ndir):
        j = lax.rem(me + s, ndir)
        copy4(j, j).wait_recv()

    for y in range(chips):
        pair = jnp.concatenate(
            [recv4[2 * y + h].astype(F32).reshape(128, 128).astype(BF16) for h in range(2)], axis=1
        )
        inc[:, y * 256 : (y + 1) * 256] = jnp.dot(perm_t, pair, preferred_element_type=F32)

    def far_step(i, carry):
        for j in range(4):
            b = 4 * i + j
            for y in range(chips):
                lanes = slice(y * 256, (y + 1) * 256)
                c = cosb[y, pl.ds(b, 1), :]
                d = sinb[y, pl.ds(b, 1), :]
                re = inc[0:64, lanes]
                im = inc[64:128, lanes]
                shf[j * 128 : j * 128 + 64, lanes] = (c * re + d * im).astype(BF16)
                shf[j * 128 + 64 : (j + 1) * 128, lanes] = (c * im - d * re).astype(BF16)
        mixed = jnp.dot(shf[...], a_ref[...], preferred_element_type=F32)
        for j in range(4):
            b = 4 * i + j
            m = mixed[j * 128 : (j + 1) * 128]
            far = jnp.concatenate(
                [m[0:64, 0:128] + m[64:128, 128:256], m[64:128, 0:128] - m[0:64, 128:256]], axis=0
            )
            out_ref[b] = (near[b] + far.T).astype(BF16)
        return carry

    lax.fori_loop(0, boxes // 4, far_step, 0)

    to_right.wait_send()
    to_left.wait_send()
    for s in range(1, ndir):
        j = lax.rem(me + s, ndir)
        copy1(j).wait_send()
        copy4(j, me).wait_send()
    for s in range(1, nbox):
        g = lax.rem(box + s, nbox)
        copy2(g, box).wait_send()
        copy3(g, box).wait_send()


def local(
    nbox,
    ndir,
    currents,
    near_blocks,
    near_list,
    near_count,
    radiation,
    child_angle,
    translation,
    inter_src,
    inter_off,
    inter_count,
):
    boxes = currents.shape[0]
    half = boxes // 2
    kn = near_list.shape[1]
    slots = inter_src.shape[1]
    first = (lax.axis_index("box") * ndir + lax.axis_index("dir")) * boxes
    live = jnp.arange(kn, dtype=jnp.int32)[None, :] < near_count[:, None]
    ids = jnp.where(live, jnp.clip(near_list - first + half, 0, 2 * boxes - 1), 2 * boxes)
    used = jnp.arange(slots, dtype=jnp.int32)[None, :] < inter_count[:, None]
    offs = jnp.where(used, jnp.clip(inter_off, 0, translation.shape[0] - 1), translation.shape[0])
    srcs = jnp.clip(inter_src, 0, nbox * ndir - 1)
    smem = pl.BlockSpec(memory_space=pltpu.SMEM)
    hbm = pl.BlockSpec(memory_space=pl.ANY)
    dma = pltpu.SemaphoreType.DMA
    return pl.pallas_call(
        functools.partial(kernel, nbox, ndir),
        out_shape=jax.ShapeDtypeStruct((boxes, 128, 128), BF16),
        in_specs=[smem] * 3 + [hbm] * 5,
        out_specs=pl.BlockSpec(memory_space=pltpu.VMEM),
        scratch_shapes=[
            pltpu.VMEM((2 * boxes + 1, 128, 128), BF16),
            pltpu.VMEM(near_blocks.shape, BF16),
            pltpu.VMEM(radiation.shape, BF16),
            pltpu.VMEM(child_angle.shape, F32),
            pltpu.VMEM((translation.shape[0] + 4, 2, 128), F32),
            pltpu.VMEM((ndir // 2, boxes, 256), F32),
            pltpu.VMEM((ndir // 2, boxes, 256), F32),
            pltpu.VMEM((boxes * 128, 256), BF16),
            pltpu.VMEM((ndir, nbox, 8, 128), BF16),
            pltpu.VMEM((ndir, nbox, 8, 128), BF16),
            pltpu.VMEM((nbox * ndir, 8, 128), BF16),
            pltpu.VMEM((nbox * ndir, 8, 128), BF16),
            pltpu.VMEM((nbox, ndir, 8, 128), BF16),
            pltpu.VMEM((ndir, nbox, 8, 128), BF16),
            pltpu.VMEM((boxes, 128, 128), F32),
            pltpu.VMEM((128, ndir * 128), F32),
            pltpu.VMEM((512, ndir * 128), BF16),
            dma((5,)),
            dma((4,)),
            dma((ndir,)),
            dma((ndir,)),
            dma((nbox,)),
            dma((nbox,)),
            dma((nbox,)),
            dma((nbox,)),
            dma((ndir,)),
            dma((ndir,)),
            dma((2,)),
            dma((2,)),
        ],
        compiler_params=pltpu.CompilerParams(
            collective_id=0, has_side_effects=True, vmem_limit_bytes=50 * 2**20
        ),
    )(
        ids.reshape(-1),
        srcs.reshape(-1),
        offs.reshape(-1),
        currents,
        near_blocks,
        radiation,
        child_angle,
        translation,
    )


def solution(mesh):
    nbox, ndir = mesh.shape["box"], mesh.shape["dir"]
    return jax.shard_map(
        functools.partial(local, nbox, ndir),
        mesh=mesh,
        in_specs=(
            P(("box", "dir"), None, None),
            P(("box", "dir"), None, None, None),
            P(("box", "dir"), None),
            P(("box", "dir")),
            P(),
            P(("box", "dir"), None),
            P(),
            P(),
            P(),
            P(),
        ),
        out_specs=P(("box", "dir"), None, None),
        check_vma=False,
    )
```

time: 187 us -> 45 us (0.24)
  the two profiles are of different devices: /device:TPU:1 before, /device:TPU:17 now
where the time goes in v1:
time: 45 us; the launch traced here: 44.6 us
  Pallas kernels  38.2 us (85%)
  local copies, waits for them, and re-layouts  4.37 us (10%)
  other arithmetic  2.08 us (5%)
    pallas_call x1, Pallas kernels, local(): pl.pallas_call(functools.partial(kernel, nbox, ndir), out_shape=jax.Shape...  38.2 us
    unnamed x7, local copies, waits for them, and re-layouts  3.71 us

profile of v1, /device:TPU:17, one launch (start us, length us, event | category | flops | bytes accessed | tf_op | source)
XLA Modules:
  0.0 44.6 jit_solution(14252804860630519873)
XLA Ops:
  0.0 0.7 %clamp_select_fusion.1 = s32[16,8]{0,1:T(8,128)S(1)} fusion(s32[16,8]{0,1:T(8,128)} %param.12, s32[]{:T(128)S(6)} %mul.7, s32[16]{0:T(128)} %param.13), kind=kLoop, calls=%fused_computation.2 | loop fusion | flops 640 | bytes 1092 | tf_op jit(solution)/shard_map/jit(_where)/select_n | solution.py:396
  0.7 0.1 copy.12
  0.8 0.1 reshape.11.ids
  0.9 0.7 %broadcast_clamp_fusion = s32[128,6]{0,1:T(8,128)S(1)} fusion(s32[128,6]{0,1:T(8,128)} %param.17), kind=kLoop, calls=%fused_computation.4 | loop fusion | flops 768 | bytes 6144 | tf_op jit(solution)/shard_map/jit(clip)/min | solution.py:399
  1.6 0.7 %clamp_select_fusion = s32[128,6]{0,1:T(8,128)S(1)} fusion(s32[128,6]{0,1:T(8,128)} %param.18, s32[128]{0:T(128)} %param.19), kind=kLoop, calls=%fused_computation | loop fusion | flops 2304 | bytes 6656 | tf_op jit(solution)/shard_map/jit(_where)/select_n | solution.py:398
  2.2 0.1 copy.14
  2.4 0.1 reshape.13.off
  2.5 0.1 copy.13
  2.6 0.1 reshape.12.src
  2.8 0.0 copy-start
  2.8 1.0 %copy-done = bf16[16,128,128]{2,1,0:T(8,128)(2,1)S(1)} copy-done((bf16[16,128,128]{2,1,0:T(8,128)(2,1)S(1)}, bf16[16,128,128]{2,1,0:T(8,128)(2,1)}, u32[]{:S(2)}) %copy-start) | copy-done | bytes 524312
  3.8 0.0 copy-start.1
  3.8 1.0 %copy-done.1 = bf16[1024,256]{1,0:T(8,128)(2,1)S(1)} copy-done((bf16[1024,256]{1,0:T(8,128)(2,1)S(1)}, bf16[1024,256]{1,0:T(8,128)(2,1)}, u32[]{:S(2)}) %copy-start.1) | copy-done | bytes 524312
  4.8 0.0 copy-start.2
  4.8 0.8 %copy-done.2 = f32[16,1024]{1,0:T(8,128)S(1)} copy-done((f32[16,1024]{1,0:T(8,128)S(1)}, f32[16,1024]{1,0:T(8,128)}, u32[]{:S(2)}) %copy-start.2) | copy-done | bytes 65560
  5.7 38.2 %shard_map.100 = bf16[16,128,128]{2,1,0:T(8,128)(2,1)S(1)} custom-call(s32[128]{0:T(128)S(1)} %reshape.11.ids, s32[768]{0:T(1024)S(1)} %reshape.12.src, s32[768]{0:T(1024)S(1)} %reshape.13.off, bf16[16,128,128]{2,1,0:T(8,128)(2,1)S(1)} %copy-done, bf16[16,8,128,256]{3,2,1,0:T(8,128)(2,1)} %z_hbm.1, bf16[1024,256]{1,0:T(8,128)(2,1)S(1)} %copy-done.1, ...), custom_call_target="tpu_custom_call" | custom-call | tf_op jit(solution)/shard_map/pallas_call | solution.py:403
  43.9 0.8 %copy.16 = bf16[16,128,128]{2,1,0:T(8,128)(2,1)} copy(bf16[16,128,128]{2,1,0:T(8,128)(2,1)S(1)} %shard_map.100) | data formatting | bytes 1048576
Async XLA Ops:
  2.8 1.0 %copy-start = (bf16[16,128,128]{2,1,0:T(8,128)(2,1)S(1)}, bf16[16,128,128]{2,1,0:T(8,128)(2,1)}, u32[]{:S(2)}) copy-start(bf16[16,128,128]{2,1,0:T(8,128)(2,1)} %x_hbm.1) | copy-start | bytes 1572868
  3.8 1.0 %copy-start.1 = (bf16[1024,256]{1,0:T(8,128)(2,1)S(1)}, bf16[1024,256]{1,0:T(8,128)(2,1)}, u32[]{:S(2)}) copy-start(bf16[1024,256]{1,0:T(8,128)(2,1)} %a_hbm.1) | copy-start | bytes 1572868
  4.8 0.8 %copy-start.2 = (f32[16,1024]{1,0:T(8,128)S(1)}, f32[16,1024]{1,0:T(8,128)}, u32[]{:S(2)}) copy-start(f32[16,1024]{1,0:T(8,128)} %ang_hbm.1) | copy-start | bytes 196612

commit v2 on v1

v2 whole, which is shorter than its diff:
```python
import functools

import jax
import jax.numpy as jnp
from jax import lax
from jax.experimental import pallas as pl
from jax.experimental.pallas import tpu as pltpu
from jax.sharding import PartitionSpec as P

LOGICAL = pl.DeviceIdType.LOGICAL
F32 = jnp.float32
BF16 = jnp.bfloat16
NT = (((1,), (1,)), ((), ()))


def sincos(angle):
    h = angle * 0.5
    z = h * h
    s = -1.0 / 1307674368000.0
    for inv in (6227020800.0, -39916800.0, 362880.0, -5040.0, 120.0, -6.0, 1.0):
        s = s * z + 1.0 / inv
    s = s * h
    c = 1.0 / 20922789888000.0
    for inv in (-87178291200.0, 479001600.0, -3628800.0, 40320.0, -720.0, 24.0, -2.0, 1.0):
        c = c * z + 1.0 / inv
    return 2.0 * s * c, 1.0 - 2.0 * s * s


def iota2(rows, columns):
    return (
        lax.broadcasted_iota(jnp.int32, (rows, columns), 0),
        lax.broadcasted_iota(jnp.int32, (rows, columns), 1),
    )


def kernel(
    nbox,
    ndir,
    list_hbm,
    count_hbm,
    src_hbm,
    off_hbm,
    used_hbm,
    x_hbm,
    z_hbm,
    a_hbm,
    ang_hbm,
    tr_hbm,
    out_hbm,
    nlist,
    ncount,
    src,
    off,
    used,
    xext,
    zbuf,
    a_ref,
    ang,
    trans,
    cosb,
    sinb,
    lhs,
    send1,
    recv1,
    send2,
    recv2,
    near,
    inc,
    shf,
    out,
    load_sem,
    table_sem,
    own_sem,
    out_sem,
    s1,
    r1,
    s2,
    r2,
    sh,
    rh,
):
    box = lax.axis_index("box")
    me = lax.axis_index("dir")
    chips = ndir // 2
    my_y = me // 2
    boxes = x_hbm.shape[0]
    half = boxes // 2
    total = nbox * ndir
    rank = box * ndir + me

    load_x = pltpu.make_async_copy(x_hbm, xext.at[pl.ds(half, boxes)], load_sem.at[0])
    load_a = pltpu.make_async_copy(a_hbm, a_ref, load_sem.at[1])
    load_g = pltpu.make_async_copy(ang_hbm, ang, load_sem.at[2])
    load_t = pltpu.make_async_copy(
        tr_hbm.at[:, :, pl.ds(pl.multiple_of(me * 128, 128), 128)],
        trans.at[pl.ds(0, tr_hbm.shape[0])],
        load_sem.at[3],
    )
    load_z = pltpu.make_async_copy(z_hbm, zbuf, load_sem.at[4])
    tables = [
        pltpu.make_async_copy(there, here, table_sem.at[i])
        for i, (there, here) in enumerate(
            (
                (list_hbm, nlist),
                (count_hbm, ncount),
                (src_hbm, src),
                (off_hbm, off),
                (used_hbm, used),
            )
        )
    ]
    load_g.start()
    load_x.start()
    load_a.start()
    load_t.start()
    for table in tables:
        table.start()
    load_z.start()

    barrier = pltpu.get_barrier_semaphore()
    for s in range(1, total):
        pl.semaphore_signal(
            barrier,
            inc=1,
            device_id=lax.rem(rank + s, total),
            device_id_type=LOGICAL,
        )

    xext[2 * boxes] = jnp.zeros((128, 128), BF16)
    trans[pl.ds(tr_hbm.shape[0], 4)] = jnp.zeros((4, 2, 128), F32)

    row, col = iota2(128, 128)
    within = lax.rem(row, 8)
    natural = 4 * lax.div(row, 8) + lax.rem(within, 4) + 64 * lax.div(within, 4)
    perm = jnp.where(col == natural, 1.0, 0.0).astype(BF16)
    within_t = lax.rem(col, 8)
    natural_t = 4 * lax.div(col, 8) + lax.rem(within_t, 4) + 64 * lax.div(within_t, 4)
    perm_t = jnp.where(row == natural_t, 1.0, 0.0).astype(BF16)
    row2, col2 = iota2(256, 128)
    spread = jnp.where(row2 == col2, 1.0, 0.0)
    spread = jnp.where((row2 >= 128) & (row2 < 192) & (col2 == row2 - 64), -1.0, spread)
    spread = jnp.where((row2 >= 192) & (col2 == row2 - 192), 1.0, spread).astype(BF16)

    load_g.wait()
    for y in range(chips):
        sn, cs = sincos(ang[:, y * 256 : (y + 1) * 256])
        sinb[y] = sn
        cosb[y] = cs

    load_x.wait()
    for i in range(boxes // 4):
        four = xext[half + 4 * i : half + 4 * i + 4].reshape(512, 128)
        turned = lax.dot_general(spread, four, NT, preferred_element_type=F32).astype(BF16)
        for j in range(4):
            rows = slice((4 * i + j) * 128, (4 * i + j + 1) * 128)
            lhs[rows, 0:128] = turned[0:128, j * 128 : (j + 1) * 128]
            lhs[rows, 128:256] = turned[128:256, j * 128 : (j + 1) * 128]

    load_a.wait()

    own1 = pltpu.make_async_copy(send1.at[me * nbox + box], recv1.at[rank], own_sem.at[0])

    def pattern_step(s, carry):
        y = lax.rem(my_y + 1 + s, chips)
        block = a_ref[pl.ds(pl.multiple_of(y * 256, 256), 256), :]
        re = jnp.zeros((64, 256), F32)
        im = jnp.zeros((64, 256), F32)
        for i in range(boxes // 4):
            terms = lax.dot_general(
                lhs[512 * i : 512 * (i + 1), :], block, NT, preferred_element_type=F32
            )
            for j in range(4):
                b = 4 * i + j
                c = cosb[y, b : b + 1, :]
                d = sinb[y, b : b + 1, :]
                tre = terms[j * 128 : j * 128 + 64]
                tim = terms[j * 128 + 64 : (j + 1) * 128]
                re = re + (c * tre - d * tim)
                im = im + (d * tre + c * tim)
        pat = jnp.concatenate([re, im], axis=0).astype(BF16)
        pat = jnp.dot(perm, pat, preferred_element_type=F32)
        for h in range(2):
            send1[pl.ds((2 * y + h) * nbox, nbox)] = (
                pat[:, h * 128 : (h + 1) * 128].reshape(nbox, 8, 128).astype(BF16)
            )

        @pl.when(s == 0)
        def _():
            pl.semaphore_wait(barrier, total - 1)

        def send(g, j):
            pltpu.make_async_remote_copy(
                src_ref=send1.at[j * nbox + g],
                dst_ref=recv1.at[rank],
                send_sem=s1,
                recv_sem=r1,
                device_id=g * ndir + j,
                device_id_type=LOGICAL,
            ).start()

        for i in range(1, nbox):
            for h in range(2):
                send(lax.rem(box + i, nbox), 2 * y + h)
        for h in range(2):
            j = 2 * y + h

            @pl.when(j != me)
            def _():
                send(box, j)

            @pl.when(j == me)
            def _():
                own1.start()

        return carry

    lax.fori_loop(0, chips, pattern_step, 0)

    to_right = pltpu.make_async_remote_copy(
        src_ref=xext.at[pl.ds(boxes, half)],
        dst_ref=xext.at[pl.ds(0, half)],
        send_sem=sh.at[0],
        recv_sem=rh.at[0],
        device_id=lax.rem(rank + 1, total),
        device_id_type=LOGICAL,
    )
    to_left = pltpu.make_async_remote_copy(
        src_ref=xext.at[pl.ds(half, half)],
        dst_ref=xext.at[pl.ds(half + boxes, half)],
        send_sem=sh.at[1],
        recv_sem=rh.at[1],
        device_id=lax.rem(rank + total - 1, total),
        device_id_type=LOGICAL,
    )
    to_right.start()
    to_left.start()

    def all_but_one(there, here, send_sem, recv_sem):
        return pltpu.make_async_remote_copy(
            src_ref=there.at[pl.ds(0, total - 1)],
            dst_ref=here.at[pl.ds(0, total - 1)],
            send_sem=send_sem,
            recv_sem=recv_sem,
            device_id=lax.rem(rank + 1, total),
            device_id_type=LOGICAL,
        )

    load_t.wait()
    for table in tables:
        table.wait()
    own1.wait()
    all_but_one(send1, recv1, s1, r1).wait_recv()

    own2 = pltpu.make_async_copy(send2.at[rank], recv2.at[me * nbox + box], own_sem.at[1])
    sign = jnp.where(lax.broadcasted_iota(jnp.int32, (8, 128), 0) < 4, -1.0, 1.0)
    slots = src.shape[1]
    nothing = tr_hbm.shape[0]

    def translate_step(s, carry):
        g = lax.rem(box + 1 + s, nbox)
        for i in range(ndir):
            t = g * ndir + i
            straight = jnp.zeros((8, 128), F32)
            crossed = jnp.zeros((8, 128), F32)
            for k in range(slots):
                v = recv1[src[t, k]].astype(F32)
                tau = trans[jnp.where(k < used[t], off[t, k], nothing)]
                straight = straight + tau[0:1] * v
                crossed = crossed + tau[1:2] * v
            total_in = straight + sign * pltpu.roll(crossed, 4, 0)
            send2[t] = total_in.astype(BF16)

        for i in range(ndir):
            t = g * ndir + i

            @pl.when(t != rank)
            def _():
                pltpu.make_async_remote_copy(
                    src_ref=send2.at[t],
                    dst_ref=recv2.at[me * nbox + box],
                    send_sem=s2,
                    recv_sem=r2,
                    device_id=t,
                    device_id_type=LOGICAL,
                ).start()

            @pl.when(t == rank)
            def _():
                own2.start()

        return carry

    lax.fori_loop(0, nbox, translate_step, 0)

    load_z.wait()
    to_right.wait_recv()
    to_left.wait_recv()
    first = rank * boxes - half

    def near_step(b, carry):
        count = ncount[b]
        gathered = jnp.concatenate(
            [xext[jnp.where(k < count, nlist[b, k] - first, 2 * boxes)] for k in range(8)], axis=0
        )
        zr = jnp.concatenate([zbuf[b, k, :, 0:128] for k in range(8)], axis=1)
        zi = jnp.concatenate([zbuf[b, k, :, 128:256] for k in range(8)], axis=1)
        both = jnp.dot(
            jnp.concatenate([zr, zi], axis=0), gathered, preferred_element_type=F32
        )
        cross = pltpu.roll(both[128:256], 64, 1)
        lane = lax.broadcasted_iota(jnp.int32, (128, 128), 1)
        near[b] = both[0:128] + jnp.where(lane < 64, -cross, cross)
        return carry

    lax.fori_loop(0, boxes, near_step, 0)

    own2.wait()
    all_but_one(send2, recv2, s2, r2).wait_recv()

    for y in range(chips):
        pair = jnp.concatenate(
            [
                recv2[(2 * y + h) * nbox : (2 * y + h + 1) * nbox]
                .astype(F32)
                .reshape(128, 128)
                .astype(BF16)
                for h in range(2)
            ],
            axis=1,
        )
        inc[:, y * 256 : (y + 1) * 256] = jnp.dot(perm_t, pair, preferred_element_type=F32)

    def write(i):
        group = pl.ds(4 * i, 4)
        return pltpu.make_async_copy(out.at[group], out_hbm.at[group], out_sem.at[i])

    def far_step(i, carry):
        for j in range(4):
            b = 4 * i + j
            for y in range(chips):
                lanes = slice(y * 256, (y + 1) * 256)
                c = cosb[y, pl.ds(b, 1), :]
                d = sinb[y, pl.ds(b, 1), :]
                re = inc[0:64, lanes]
                im = inc[64:128, lanes]
                shf[j * 128 : j * 128 + 64, lanes] = (c * re + d * im).astype(BF16)
                shf[j * 128 + 64 : (j + 1) * 128, lanes] = (c * im - d * re).astype(BF16)
        mixed = jnp.dot(shf[...], a_ref[...], preferred_element_type=F32)
        for j in range(4):
            b = 4 * i + j
            m = mixed[j * 128 : (j + 1) * 128]
            far = jnp.concatenate(
                [m[0:64, 0:128] + m[64:128, 128:256], m[64:128, 0:128] - m[0:64, 128:256]], axis=0
            )
            out[b] = (near[b] + far.T).astype(BF16)
        write(i).start()
        return carry

    lax.fori_loop(0, boxes // 4, far_step, 0)

    to_right.wait_send()
    to_left.wait_send()
    all_but_one(send1, recv1, s1, r1).wait_send()
    all_but_one(send2, recv2, s2, r2).wait_send()
    for i in range(boxes // 4):
        write(i).wait()


def local(
    nbox,
    ndir,
    currents,
    near_blocks,
    near_list,
    near_count,
    radiation,
    child_angle,
    translation,
    inter_src,
    inter_off,
    inter_count,
):
    boxes = currents.shape[0]
    total = nbox * ndir
    hbm = pl.BlockSpec(memory_space=pl.ANY)
    dma = pltpu.SemaphoreType.DMA
    return pl.pallas_call(
        functools.partial(kernel, nbox, ndir),
        out_shape=jax.ShapeDtypeStruct((boxes, 128, 128), BF16),
        in_specs=[hbm] * 10,
        out_specs=hbm,
        scratch_shapes=[
            pltpu.SMEM(near_list.shape, jnp.int32),
            pltpu.SMEM(near_count.shape, jnp.int32),
            pltpu.SMEM(inter_src.shape, jnp.int32),
            pltpu.SMEM(inter_off.shape, jnp.int32),
            pltpu.SMEM(inter_count.shape, jnp.int32),
            pltpu.VMEM((2 * boxes + 1, 128, 128), BF16),
            pltpu.VMEM(near_blocks.shape, BF16),
            pltpu.VMEM(radiation.shape, BF16),
            pltpu.VMEM(child_angle.shape, F32),
            pltpu.VMEM((translation.shape[0] + 4, 2, 128), F32),
            pltpu.VMEM((ndir // 2, boxes, 256), F32),
            pltpu.VMEM((ndir // 2, boxes, 256), F32),
            pltpu.VMEM((boxes * 128, 256), BF16),
            pltpu.VMEM((total, 8, 128), BF16),
            pltpu.VMEM((total, 8, 128), BF16),
            pltpu.VMEM((total, 8, 128), BF16),
            pltpu.VMEM((total, 8, 128), BF16),
            pltpu.VMEM((boxes, 128, 128), F32),
            pltpu.VMEM((128, ndir * 128), F32),
            pltpu.VMEM((512, ndir * 128), BF16),
            pltpu.VMEM((boxes, 128, 128), BF16),
            dma((5,)),
            dma((5,)),
            dma((2,)),
            dma((boxes // 4,)),
            dma,
            dma,
            dma,
            dma,
            dma((2,)),
            dma((2,)),
        ],
        compiler_params=pltpu.CompilerParams(
            collective_id=0, has_side_effects=True, vmem_limit_bytes=60 * 2**20
        ),
    )(
        near_list,
        near_count,
        inter_src,
        inter_off,
        inter_count,
        currents,
        near_blocks,
        radiation,
        child_angle,
        translation,
    )


def solution(mesh):
    nbox, ndir = mesh.shape["box"], mesh.shape["dir"]
    return jax.shard_map(
        functools.partial(local, nbox, ndir),
        mesh=mesh,
        in_specs=(
            P(("box", "dir"), None, None),
            P(("box", "dir"), None, None, None),
            P(("box", "dir"), None),
            P(("box", "dir")),
            P(),
            P(("box", "dir"), None),
            P(),
            P(),
            P(),
            P(),
        ),
        out_specs=P(("box", "dir"), None, None),
        check_vma=False,
    )
```

time: 45 us -> 38 us (0.84)
  the two profiles are of different devices: /device:TPU:17 before, /device:TPU:1 now
where the time goes in v2:
time: 38 us; the launch traced here: 37.3 us
  Pallas kernels  31.2 us (82%)
  local copies, waits for them, and re-layouts  6.07 us (16%)
    pallas_call x1, Pallas kernels, local(): pl.pallas_call(functools.partial(kernel, nbox, ndir), out_shape=jax.Shape...  31.2 us
    unnamed x4, local copies, waits for them, and re-layouts  6.07 us

profile of v2, /device:TPU:1, one launch (start us, length us, event | category | flops | bytes accessed | tf_op | source)
XLA Modules:
  0.0 37.3 jit_solution(17515356384298949581)
XLA Ops:
  0.0 1.4 %copy.11.list_hbm = s32[16,8]{1,0:T(8,128)} copy(s32[16,8]{0,1:T(8,128)} %param.12) | data formatting | bytes 1024 | tf_op args[2]
  1.4 1.4 %copy.12.src_hbm = s32[128,6]{1,0:T(8,128)} copy(s32[128,6]{0,1:T(8,128)} %param.17) | data formatting | bytes 6144 | tf_op args[7]
  2.8 1.4 %copy.13.off_hbm = s32[128,6]{1,0:T(8,128)} copy(s32[128,6]{0,1:T(8,128)} %param.18) | data formatting | bytes 6144 | tf_op args[8]
  4.2 31.2 %shard_map.100 = bf16[16,128,128]{2,1,0:T(8,128)(2,1)} custom-call(s32[16,8]{1,0:T(8,128)} %copy.11.list_hbm, s32[16]{0:T(128)} %count_hbm.1, s32[128,6]{1,0:T(8,128)} %copy.12.src_hbm, s32[128,6]{1,0:T(8,128)} %copy.13.off_hbm, s32[128]{0:T(128)} %used_hbm.1, bf16[16,128,128]{2,1,0:T(8,128)(2,1)} %x_hbm.1, bf16[16,8,128,256]{3,2,1,0:T(8,128)(2,1)} %z_hbm.1, ...), custom_call_target="tpu_custom_call" | custom-call | tf_op jit(solution)/shard_map/pallas_call | solution.py:387
  35.4 1.9 %copy.15 = bf16[16,128,128]{2,1,0:T(8,128)(2,1)} copy(bf16[16,128,128]{2,1,0:T(8,128)(2,1)} %shard_map.100) | data formatting | bytes 1048576

commit v3 on v2

--- a/solution.py
+++ b/solution.py
@@ -24,6 +24,13 @@
     for inv in (-87178291200.0, 479001600.0, -3628800.0, 40320.0, -720.0, 24.0, -2.0, 1.0):
         c = c * z + 1.0 / inv
     return 2.0 * s * c, 1.0 - 2.0 * s * s
+
+
+def far_groups(side):
+    return sorted(
+        ((z, x) for z in range(side) for x in range(side)),
+        key=lambda o: -min(o[0], side - o[0]) - min(o[1], side - o[1]),
+    )
 
 
 def iota2(rows, columns):
@@ -46,13 +53,14 @@
     a_hbm,
     ang_hbm,
     tr_hbm,
-    out_hbm,
+    out,
     nlist,
     ncount,
     src,
     off,
     used,
-    xext,
+    xsib,
+    xoth,
     zbuf,
     a_ref,
     ang,
@@ -67,11 +75,9 @@
     near,
     inc,
     shf,
-    out,
     load_sem,
     table_sem,
     own_sem,
-    out_sem,
     s1,
     r1,
     s2,
@@ -82,13 +88,30 @@
     box = lax.axis_index("box")
     me = lax.axis_index("dir")
     chips = ndir // 2
+    side = round(nbox**0.5)
+    box_z, box_x = box // side, lax.rem(box, side)
+
+    def group_at(offset):
+        return lax.rem(box_z + offset[0], side) * side + lax.rem(box_x + offset[1], side)
+
     my_y = me // 2
+    core = lax.rem(me, 2)
     boxes = x_hbm.shape[0]
     half = boxes // 2
     total = nbox * ndir
     rank = box * ndir + me
 
-    load_x = pltpu.make_async_copy(x_hbm, xext.at[pl.ds(half, boxes)], load_sem.at[0])
+    barrier = pltpu.get_barrier_semaphore()
+    for there in range(1, total):
+        pl.semaphore_signal(
+            barrier,
+            inc=1,
+            device_id=lax.rem(rank + there, total),
+            device_id_type=LOGICAL,
+        )
+
+    load_x = pltpu.make_async_copy(x_hbm, xsib.at[pl.ds(core * half, boxes)], load_sem.at[0])
+    load_o = pltpu.make_async_copy(x_hbm, xoth.at[pl.ds((1 - core) * half, boxes)], load_sem.at[5])
     load_a = pltpu.make_async_copy(a_hbm, a_ref, load_sem.at[1])
     load_g = pltpu.make_async_copy(ang_hbm, ang, load_sem.at[2])
     load_t = pltpu.make_async_copy(
@@ -112,21 +135,14 @@
     load_g.start()
     load_x.start()
     load_a.start()
+    load_o.start()
     load_t.start()
     for table in tables:
         table.start()
     load_z.start()
 
-    barrier = pltpu.get_barrier_semaphore()
-    for s in range(1, total):
-        pl.semaphore_signal(
-            barrier,
-            inc=1,
-            device_id=lax.rem(rank + s, total),
-            device_id_type=LOGICAL,
-        )
-
-    xext[2 * boxes] = jnp.zeros((128, 128), BF16)
+    xsib[boxes + half] = jnp.zeros((128, 128), BF16)
+    xoth[boxes + half] = jnp.zeros((128, 128), BF16)
     trans[pl.ds(tr_hbm.shape[0], 4)] = jnp.zeros((4, 2, 128), F32)
 
     row, col = iota2(128, 128)
@@ -149,7 +165,7 @@
 
     load_x.wait()
     for i in range(boxes // 4):
-        four = xext[half + 4 * i : half + 4 * i + 4].reshape(512, 128)
+        four = xsib[pl.ds(core * half + 4 * i, 4)].reshape(512, 128)
         turned = lax.dot_general(spread, four, NT, preferred_element_type=F32).astype(BF16)
         for j in range(4):
             rows = slice((4 * i + j) * 128, (4 * i + j + 1) * 128)
@@ -157,11 +173,29 @@
             lhs[rows, 128:256] = turned[128:256, j * 128 : (j + 1) * 128]
 
     load_a.wait()
+    load_o.wait()
 
     own1 = pltpu.make_async_copy(send1.at[me * nbox + box], recv1.at[rank], own_sem.at[0])
 
+    to_sibling = pltpu.make_async_remote_copy(
+        src_ref=xsib.at[pl.ds(half, half)],
+        dst_ref=xsib.at[pl.ds(core * boxes, half)],
+        send_sem=sh.at[0],
+        recv_sem=rh.at[0],
+        device_id=rank + 1 - 2 * core,
+        device_id_type=LOGICAL,
+    )
+    to_other = pltpu.make_async_remote_copy(
+        src_ref=xoth.at[pl.ds(half, half)],
+        dst_ref=xoth.at[pl.ds((1 - core) * boxes, half)],
+        send_sem=sh.at[1],
+        recv_sem=rh.at[1],
+        device_id=lax.rem(rank + total - 1 + 2 * core, total),
+        device_id_type=LOGICAL,
+    )
+
     def pattern_step(s, carry):
-        y = lax.rem(my_y + 1 + s, chips)
+        y = lax.rem(my_y + jnp.where(s == 0, 2, jnp.where(s == 1, 1, jnp.where(s == 2, 3, 0))), chips)
         block = a_ref[pl.ds(pl.multiple_of(y * 256, 256), 256), :]
         re = jnp.zeros((64, 256), F32)
         im = jnp.zeros((64, 256), F32)
@@ -187,6 +221,7 @@
         @pl.when(s == 0)
         def _():
             pl.semaphore_wait(barrier, total - 1)
+            to_sibling.start()
 
         def send(g, j):
             pltpu.make_async_remote_copy(
@@ -198,9 +233,9 @@
                 device_id_type=LOGICAL,
             ).start()
 
-        for i in range(1, nbox):
+        for offset in far_groups(side)[:-1]:
             for h in range(2):
-                send(lax.rem(box + i, nbox), 2 * y + h)
+                send(group_at(offset), 2 * y + h)
         for h in range(2):
             j = 2 * y + h
 
@@ -216,24 +251,7 @@
 
     lax.fori_loop(0, chips, pattern_step, 0)
 
-    to_right = pltpu.make_async_remote_copy(
-        src_ref=xext.at[pl.ds(boxes, half)],
-        dst_ref=xext.at[pl.ds(0, half)],
-        send_sem=sh.at[0],
-        recv_sem=rh.at[0],
-        device_id=lax.rem(rank + 1, total),
-        device_id_type=LOGICAL,
-    )
-    to_left = pltpu.make_async_remote_copy(
-        src_ref=xext.at[pl.ds(half, half)],
-        dst_ref=xext.at[pl.ds(half + boxes, half)],
-        send_sem=sh.at[1],
-        recv_sem=rh.at[1],
-        device_id=lax.rem(rank + total - 1, total),
-        device_id_type=LOGICAL,
-    )
-    to_right.start()
-    to_left.start()
+    to_other.start()
 
     def all_but_one(there, here, send_sem, recv_sem):
         return pltpu.make_async_remote_copy(
@@ -245,26 +263,58 @@
             device_id_type=LOGICAL,
         )
 
-    load_t.wait()
+    def near_box(x, own, b):
+        count = ncount[b]
+        gathered = jnp.concatenate(
+            [
+                x[jnp.where(k < count, nlist[k, b] - rank * boxes + own, boxes + half)]
+                for k in range(8)
+            ],
+            axis=0,
+        )
+        zr = jnp.concatenate([zbuf[b, k, :, 0:128] for k in range(8)], axis=1)
+        zi = jnp.concatenate([zbuf[b, k, :, 128:256] for k in range(8)], axis=1)
+        both = jnp.dot(
+            jnp.concatenate([zr, zi], axis=0), gathered, preferred_element_type=F32
+        )
+        cross = pltpu.roll(both[128:256], 64, 1)
+        lane = lax.broadcasted_iota(jnp.int32, (128, 128), 1)
+        near[b] = both[0:128] + jnp.where(lane < 64, -cross, cross)
+
+    def near_sibling(i, carry):
+        near_box(xsib, core * half, (1 - core) * half + i)
+        return carry
+
+    load_z.wait()
     for table in tables:
         table.wait()
+    to_sibling.wait_recv()
+    lax.fori_loop(0, half, near_sibling, 0)
+
+    load_t.wait()
     own1.wait()
     all_but_one(send1, recv1, s1, r1).wait_recv()
 
     own2 = pltpu.make_async_copy(send2.at[rank], recv2.at[me * nbox + box], own_sem.at[1])
     sign = jnp.where(lax.broadcasted_iota(jnp.int32, (8, 128), 0) < 4, -1.0, 1.0)
-    slots = src.shape[1]
+    slots = src.shape[0]
     nothing = tr_hbm.shape[0]
 
-    def translate_step(s, carry):
-        g = lax.rem(box + 1 + s, nbox)
+    def group_of(s):
+        code = sum(
+            jnp.where(s == i, z * side + x, 0) for i, (z, x) in enumerate(far_groups(side))
+        )
+        return group_at((code // side, lax.rem(code, side)))
+
+    def translate_group(s):
+        g = group_of(s)
         for i in range(ndir):
             t = g * ndir + i
             straight = jnp.zeros((8, 128), F32)
             crossed = jnp.zeros((8, 128), F32)
             for k in range(slots):
-                v = recv1[src[t, k]].astype(F32)
-                tau = trans[jnp.where(k < used[t], off[t, k], nothing)]
+                v = recv1[src[k, t]].astype(F32)
+                tau = trans[jnp.where(k < used[t], off[k, t], nothing)]
                 straight = straight + tau[0:1] * v
                 crossed = crossed + tau[1:2] * v
             total_in = straight + sign * pltpu.roll(crossed, 4, 0)
@@ -288,31 +338,19 @@
             def _():
                 own2.start()
 
+
+    def translate_step(s, carry):
+        translate_group(s)
         return carry
 
-    lax.fori_loop(0, nbox, translate_step, 0)
-
-    load_z.wait()
-    to_right.wait_recv()
-    to_left.wait_recv()
-    first = rank * boxes - half
-
-    def near_step(b, carry):
-        count = ncount[b]
-        gathered = jnp.concatenate(
-            [xext[jnp.where(k < count, nlist[b, k] - first, 2 * boxes)] for k in range(8)], axis=0
-        )
-        zr = jnp.concatenate([zbuf[b, k, :, 0:128] for k in range(8)], axis=1)
-        zi = jnp.concatenate([zbuf[b, k, :, 128:256] for k in range(8)], axis=1)
-        both = jnp.dot(
-            jnp.concatenate([zr, zi], axis=0), gathered, preferred_element_type=F32
-        )
-        cross = pltpu.roll(both[128:256], 64, 1)
-        lane = lax.broadcasted_iota(jnp.int32, (128, 128), 1)
-        near[b] = both[0:128] + jnp.where(lane < 64, -cross, cross)
+    def mixed_step(i, carry):
+        near_box(xoth, (1 - core) * half, core * half + i)
+        translate_group(nbox // 2 + i)
         return carry
 
-    lax.fori_loop(0, boxes, near_step, 0)
+    lax.fori_loop(0, nbox // 2, translate_step, 0)
+    to_other.wait_recv()
+    lax.fori_loop(0, half, mixed_step, 0)
 
     own2.wait()
     all_but_one(send2, recv2, s2, r2).wait_recv()
@@ -330,22 +368,18 @@
         )
         inc[:, y * 256 : (y + 1) * 256] = jnp.dot(perm_t, pair, preferred_element_type=F32)
 
-    def write(i):
-        group = pl.ds(4 * i, 4)
-        return pltpu.make_async_copy(out.at[group], out_hbm.at[group], out_sem.at[i])
-
-    def far_step(i, carry):
+    for i in range(boxes // 4):
         for j in range(4):
             b = 4 * i + j
             for y in range(chips):
                 lanes = slice(y * 256, (y + 1) * 256)
-                c = cosb[y, pl.ds(b, 1), :]
-                d = sinb[y, pl.ds(b, 1), :]
+                c = cosb[y, b : b + 1, :]
+                d = sinb[y, b : b + 1, :]
                 re = inc[0:64, lanes]
                 im = inc[64:128, lanes]
-                shf[j * 128 : j * 128 + 64, lanes] = (c * re + d * im).astype(BF16)
-                shf[j * 128 + 64 : (j + 1) * 128, lanes] = (c * im - d * re).astype(BF16)
-        mixed = jnp.dot(shf[...], a_ref[...], preferred_element_type=F32)
+                shf[i, j * 128 : j * 128 + 64, lanes] = (c * re + d * im).astype(BF16)
+                shf[i, j * 128 + 64 : (j + 1) * 128, lanes] = (c * im - d * re).astype(BF16)
+        mixed = jnp.dot(shf[i], a_ref[...], preferred_element_type=F32)
         for j in range(4):
             b = 4 * i + j
             m = mixed[j * 128 : (j + 1) * 128]
@@ -353,17 +387,11 @@
                 [m[0:64, 0:128] + m[64:128, 128:256], m[64:128, 0:128] - m[0:64, 128:256]], axis=0
             )
             out[b] = (near[b] + far.T).astype(BF16)
-        write(i).start()
-        return carry
-
-    lax.fori_loop(0, boxes // 4, far_step, 0)
-
-    to_right.wait_send()
-    to_left.wait_send()
+
+    to_sibling.wait_send()
+    to_other.wait_send()
     all_but_one(send1, recv1, s1, r1).wait_send()
     all_but_one(send2, recv2, s2, r2).wait_send()
-    for i in range(boxes // 4):
-        write(i).wait()
 
 
 def local(
@@ -382,20 +410,21 @@
 ):
     boxes = currents.shape[0]
     total = nbox * ndir
-    hbm = pl.BlockSpec(memory_space=pl.ANY)
+    hbm = pl.BlockSpec(memory_space=pltpu.HBM)
     dma = pltpu.SemaphoreType.DMA
     return pl.pallas_call(
         functools.partial(kernel, nbox, ndir),
-        out_shape=jax.ShapeDtypeStruct((boxes, 128, 128), BF16),
+        out_shape=pltpu.VMEM((boxes, 128, 128), BF16),
         in_specs=[hbm] * 10,
-        out_specs=hbm,
+        out_specs=pl.BlockSpec(memory_space=pltpu.VMEM),
         scratch_shapes=[
-            pltpu.SMEM(near_list.shape, jnp.int32),
+            pltpu.SMEM(near_list.shape[::-1], jnp.int32),
             pltpu.SMEM(near_count.shape, jnp.int32),
-            pltpu.SMEM(inter_src.shape, jnp.int32),
-            pltpu.SMEM(inter_off.shape, jnp.int32),
+            pltpu.SMEM(inter_src.shape[::-1], jnp.int32),
+            pltpu.SMEM(inter_off.shape[::-1], jnp.int32),
             pltpu.SMEM(inter_count.shape, jnp.int32),
-            pltpu.VMEM((2 * boxes + 1, 128, 128), BF16),
+            pltpu.VMEM((3 * boxes // 2 + 1, 128, 128), BF16),
+            pltpu.VMEM((3 * boxes // 2 + 1, 128, 128), BF16),
             pltpu.VMEM(near_blocks.shape, BF16),
             pltpu.VMEM(radiation.shape, BF16),
             pltpu.VMEM(child_angle.shape, F32),
@@ -409,12 +438,10 @@
             pltpu.VMEM((total, 8, 128), BF16),
             pltpu.VMEM((boxes, 128, 128), F32),
             pltpu.VMEM((128, ndir * 128), F32),
-            pltpu.VMEM((512, ndir * 128), BF16),
-            pltpu.VMEM((boxes, 128, 128), BF16),
-            dma((5,)),
+            pltpu.VMEM((boxes // 4, 512, ndir * 128), BF16),
+            dma((6,)),
             dma((5,)),
             dma((2,)),
-            dma((boxes // 4,)),
             dma,
             dma,
             dma,
@@ -423,13 +450,13 @@
             dma((2,)),
         ],
         compiler_params=pltpu.CompilerParams(
-            collective_id=0, has_side_effects=True, vmem_limit_bytes=60 * 2**20
+            collective_id=0, has_side_effects=True, vmem_limit_bytes=57 * 2**20
         ),
     )(
-        near_list,
+        near_list.T,
         near_count,
-        inter_src,
-        inter_off,
+        inter_src.T,
+        inter_off.T,
         inter_count,
         currents,
         near_blocks,

time: 38 us -> 30.9 us (0.81); the launches traced: 37.3 us -> 30.8 us
  local copies, waits for them, and re-layouts: 6.07 us -> 0.8 us
  Pallas kernels: 31.2 us -> 30 us
    unnamed x4 -> x1, local copies, waits for them, and re-layouts: 6.07 us -> 0.8 us
    pallas_call x1, Pallas kernels: 31.2 us -> 30 us  [local(): pl.pallas_call(functools.partial(kernel, nbox, ndir), out_shape=pltpu.VME...]
where the time goes in v3:
time: 30.9 us; the launch traced here: 30.8 us
  Pallas kernels  30 us (97%)
  local copies, waits for them, and re-layouts  0.8 us (3%)
    pallas_call x1, Pallas kernels, local(): pl.pallas_call(functools.partial(kernel, nbox, ndir), out_shape=pltpu.VME...  30 us
    unnamed x1, local copies, waits for them, and re-layouts  0.8 us

profile of v3, /device:TPU:1, one launch (start us, length us, event | category | flops | bytes accessed | tf_op | source)
XLA Modules:
  0.0 30.8 jit_solution(13028595890530617995)
XLA Ops:
  0.0 30.0 %shard_map.100 = bf16[16,128,128]{2,1,0:T(8,128)(2,1)S(1)} custom-call(s32[8,16]{1,0:T(8,128)} %bitcast.3, s32[16]{0:T(128)} %count_hbm.1, s32[6,128]{1,0:T(8,128)} %bitcast.4, s32[6,128]{1,0:T(8,128)} %bitcast.5, s32[128]{0:T(128)} %used_hbm.1, bf16[16,128,128]{2,1,0:T(8,128)(2,1)} %x_hbm.1, bf16[16,8,128,256]{3,2,1,0:T(8,128)(2,1)} %z_hbm.1, ...), custom_call_target="tpu_custom_call" | custom-call | tf_op jit(solution)/shard_map/pallas_call | solution.py:415
  30.0 0.8 %copy.12 = bf16[16,128,128]{2,1,0:T(8,128)(2,1)} copy(bf16[16,128,128]{2,1,0:T(8,128)(2,1)S(1)} %shard_map.100) | data formatting | bytes 1048576

commit v4 on v3

--- a/solution.py
+++ b/solution.py
@@ -343,14 +343,13 @@
         translate_group(s)
         return carry
 
-    def mixed_step(i, carry):
+    def near_other(i, carry):
         near_box(xoth, (1 - core) * half, core * half + i)
-        translate_group(nbox // 2 + i)
         return carry
 
-    lax.fori_loop(0, nbox // 2, translate_step, 0)
+    lax.fori_loop(0, nbox, translate_step, 0)
     to_other.wait_recv()
-    lax.fori_loop(0, half, mixed_step, 0)
+    lax.fori_loop(0, half, near_other, 0)
 
     own2.wait()
     all_but_one(send2, recv2, s2, r2).wait_recv()

time: 30.9 us -> 28.8 us (0.932)
  Pallas kernels: 30 us -> 27.9 us
    pallas_call x1, Pallas kernels: 30 us -> 27.9 us  [local(): pl.pallas_call(functools.partial(kernel, nbox, ndir), out_shape=pltpu.VME...]
where the time goes in v4:
time: 28.8 us; the launch traced here: 28.7 us
  Pallas kernels  27.9 us (97%)
  local copies, waits for them, and re-layouts  0.8 us (3%)
    pallas_call x1, Pallas kernels, local(): pl.pallas_call(functools.partial(kernel, nbox, ndir), out_shape=pltpu.VME...  27.9 us
    unnamed x1, local copies, waits for them, and re-layouts  0.8 us

profile of v4, /device:TPU:1, one launch (start us, length us, event | category | flops | bytes accessed | tf_op | source)
XLA Modules:
  0.0 28.7 jit_solution(17114070764200563207)
XLA Ops:
  0.0 27.9 %shard_map.100 = bf16[16,128,128]{2,1,0:T(8,128)(2,1)S(1)} custom-call(s32[8,16]{1,0:T(8,128)} %bitcast.3, s32[16]{0:T(128)} %count_hbm.1, s32[6,128]{1,0:T(8,128)} %bitcast.4, s32[6,128]{1,0:T(8,128)} %bitcast.5, s32[128]{0:T(128)} %used_hbm.1, bf16[16,128,128]{2,1,0:T(8,128)(2,1)} %x_hbm.1, bf16[16,8,128,256]{3,2,1,0:T(8,128)(2,1)} %z_hbm.1, ...), custom_call_target="tpu_custom_call" | custom-call | tf_op jit(solution)/shard_map/pallas_call | solution.py:414
  27.9 0.8 %copy.12 = bf16[16,128,128]{2,1,0:T(8,128)(2,1)} copy(bf16[16,128,128]{2,1,0:T(8,128)(2,1)S(1)} %shard_map.100) | data formatting | bytes 1048576

commit v5 on v4

--- a/solution.py
+++ b/solution.py
@@ -59,6 +59,7 @@
     src,
     off,
     used,
+    op,
     xsib,
     xoth,
     zbuf,
@@ -102,13 +103,14 @@
     rank = box * ndir + me
 
     barrier = pltpu.get_barrier_semaphore()
-    for there in range(1, total):
-        pl.semaphore_signal(
-            barrier,
-            inc=1,
-            device_id=lax.rem(rank + there, total),
-            device_id_type=LOGICAL,
-        )
+    groups = [group_at(offset) for offset in far_groups(side)]
+    peers = [lax.rem(me + 2 * k + c, ndir) for k in (2, 1, 3, 0) for c in range(2)]
+    for d in peers:
+        for g in groups:
+            if d is not peers[-2] or g is not groups[-1]:
+                pl.semaphore_signal(
+                    barrier, inc=1, device_id=g * ndir + d, device_id_type=LOGICAL
+                )
 
     load_x = pltpu.make_async_copy(x_hbm, xsib.at[pl.ds(core * half, boxes)], load_sem.at[0])
     load_o = pltpu.make_async_copy(x_hbm, xoth.at[pl.ds((1 - core) * half, boxes)], load_sem.at[5])
@@ -233,9 +235,9 @@
                 device_id_type=LOGICAL,
             ).start()
 
-        for offset in far_groups(side)[:-1]:
+        for g in groups[:-1]:
             for h in range(2):
-                send(group_at(offset), 2 * y + h)
+                send(g, 2 * y + h)
         for h in range(2):
             j = 2 * y + h
 
@@ -285,9 +287,18 @@
         near_box(xsib, core * half, (1 - core) * half + i)
         return carry
 
-    load_z.wait()
     for table in tables:
         table.wait()
+    slots = src.shape[0]
+    nothing = tr_hbm.shape[0]
+
+    def live_step(t, carry):
+        for k in range(slots):
+            op[k, t] = jnp.where(k < used[t], off[k, t], nothing)
+        return carry
+
+    lax.fori_loop(0, total, live_step, 0, unroll=4)
+    load_z.wait()
     to_sibling.wait_recv()
     lax.fori_loop(0, half, near_sibling, 0)
 
@@ -297,8 +308,6 @@
 
     own2 = pltpu.make_async_copy(send2.at[rank], recv2.at[me * nbox + box], own_sem.at[1])
     sign = jnp.where(lax.broadcasted_iota(jnp.int32, (8, 128), 0) < 4, -1.0, 1.0)
-    slots = src.shape[0]
-    nothing = tr_hbm.shape[0]
 
     def group_of(s):
         code = sum(
@@ -314,7 +323,7 @@
             crossed = jnp.zeros((8, 128), F32)
             for k in range(slots):
                 v = recv1[src[k, t]].astype(F32)
-                tau = trans[jnp.where(k < used[t], off[k, t], nothing)]
+                tau = trans[op[k, t]]
                 straight = straight + tau[0:1] * v
                 crossed = crossed + tau[1:2] * v
             total_in = straight + sign * pltpu.roll(crossed, 4, 0)
@@ -422,6 +431,7 @@
             pltpu.SMEM(inter_src.shape[::-1], jnp.int32),
             pltpu.SMEM(inter_off.shape[::-1], jnp.int32),
             pltpu.SMEM(inter_count.shape, jnp.int32),
+            pltpu.SMEM(inter_off.shape[::-1], jnp.int32),
             pltpu.VMEM((3 * boxes // 2 + 1, 128, 128), BF16),
             pltpu.VMEM((3 * boxes // 2 + 1, 128, 128), BF16),
             pltpu.VMEM(near_blocks.shape, BF16),

time: 28.8 us -> 28.2 us (0.979)
  Pallas kernels: 27.9 us -> 27.3 us
    pallas_call x1, Pallas kernels: 27.9 us -> 27.3 us  [local(): pl.pallas_call(functools.partial(kernel, nbox, ndir), out_shape=pltpu.VME...]
where the time goes in v5:
time: 28.2 us; the launch traced here: 28.1 us
  Pallas kernels  27.3 us (97%)
  local copies, waits for them, and re-layouts  0.8 us (3%)
    pallas_call x1, Pallas kernels, local(): pl.pallas_call(functools.partial(kernel, nbox, ndir), out_shape=pltpu.VME...  27.3 us
    unnamed x1, local copies, waits for them, and re-layouts  0.8 us

profile of v5, /device:TPU:1, one launch (start us, length us, event | category | flops | bytes accessed | tf_op | source)
XLA Modules:
  0.0 28.1 jit_solution(9013470857879092006)
XLA Ops:
  0.0 27.3 %shard_map.100 = bf16[16,128,128]{2,1,0:T(8,128)(2,1)S(1)} custom-call(s32[8,16]{1,0:T(8,128)} %bitcast.3, s32[16]{0:T(128)} %count_hbm.1, s32[6,128]{1,0:T(8,128)} %bitcast.4, s32[6,128]{1,0:T(8,128)} %bitcast.5, s32[128]{0:T(128)} %used_hbm.1, bf16[16,128,128]{2,1,0:T(8,128)(2,1)} %x_hbm.1, bf16[16,8,128,256]{3,2,1,0:T(8,128)(2,1)} %z_hbm.1, ...), custom_call_target="tpu_custom_call" | custom-call | tf_op jit(solution)/shard_map/pallas_call | solution.py:423
  27.3 0.8 %copy.12 = bf16[16,128,128]{2,1,0:T(8,128)(2,1)} copy(bf16[16,128,128]{2,1,0:T(8,128)(2,1)S(1)} %shard_map.100) | data formatting | bytes 1048576

commit v6 on v5

--- a/solution.py
+++ b/solution.py
@@ -328,9 +328,6 @@
                 crossed = crossed + tau[1:2] * v
             total_in = straight + sign * pltpu.roll(crossed, 4, 0)
             send2[t] = total_in.astype(BF16)
-
-        for i in range(ndir):
-            t = g * ndir + i
 
             @pl.when(t != rank)
             def _():

time: 28.2 us -> 27.9 us (0.989)
  Pallas kernels: 27.3 us -> 27 us
where the time goes in v6:
time: 27.9 us; the launch traced here: 27.8 us
  Pallas kernels  27 us (97%)
  local copies, waits for them, and re-layouts  0.8 us (3%)
    pallas_call x1, Pallas kernels, local(): pl.pallas_call(functools.partial(kernel, nbox, ndir), out_shape=pltpu.VME...  27 us
    unnamed x1, local copies, waits for them, and re-layouts  0.8 us

profile of v6, /device:TPU:1, one launch (start us, length us, event | category | flops | bytes accessed | tf_op | source)
XLA Modules:
  0.0 27.8 jit_solution(13846988603815908405)
XLA Ops:
  0.0 27.0 %shard_map.100 = bf16[16,128,128]{2,1,0:T(8,128)(2,1)S(1)} custom-call(s32[8,16]{1,0:T(8,128)} %bitcast.3, s32[16]{0:T(128)} %count_hbm.1, s32[6,128]{1,0:T(8,128)} %bitcast.4, s32[6,128]{1,0:T(8,128)} %bitcast.5, s32[128]{0:T(128)} %used_hbm.1, bf16[16,128,128]{2,1,0:T(8,128)(2,1)} %x_hbm.1, bf16[16,8,128,256]{3,2,1,0:T(8,128)(2,1)} %z_hbm.1, ...), custom_call_target="tpu_custom_call" | custom-call | tf_op jit(solution)/shard_map/pallas_call | solution.py:420
  27.0 0.8 %copy.12 = bf16[16,128,128]{2,1,0:T(8,128)(2,1)} copy(bf16[16,128,128]{2,1,0:T(8,128)(2,1)S(1)} %shard_map.100) | data formatting | bytes 1048576
